TPU v7x, 32 devices: a whole 2x2x4 slice. The times are simulated.
32 devices in a mesh: slab: 2 (over y), tm: 8 (over z, x), space: 2 (over core).
Axes of the slice: x: 2, y: 2, z: 4, core: 2. Of those that a mesh axis runs over, the one named last changes fastest.
Arguments:
- snaps: float32 [128, 8192], P('tm', ('slab', 'space')), parts along dimension 1, may hold values from -6 to 6
- weights: float32 [8192], P(('slab', 'space')), parts along dimension 0, may hold values from 0.00012207031 to 0.0009765625
Outputs:
- gram: float32 [256, 128], P(('slab', 'tm', 'space')), parts along dimension 0
There are 2 independent parts, one for each index of `slab`. A program takes and returns all parts, laid end to end along the dimension named above; each array names one. Nothing has to cross between parts.
All inputs are finite; a program needn't handle non-finite values.
Results may differ from a plain program's by a relative error of at most 0.000067.
Values sent between devices are 32-bit elements; how exact they have to be, the bound alone decides.
A program may use at most 64 MiB of HBM per device.

v0:
```python
import jax
import jax.numpy as jnp
from jax import lax
from jax.sharding import PartitionSpec as P


def from_behind(block, axis, distance):
    devices = range(lax.axis_size(axis))
    route = [((i - distance) % len(devices), i) for i in devices]
    return lax.ppermute(block, axis, route)


def on_device(snaps, weights):
    snap_cols = snaps.shape[0]
    half_rows = snap_cols // 2
    cycle_size = lax.axis_size("tm")
    position = lax.axis_index("tm")
    halfway = cycle_size // 2
    weighted = snaps * weights[None, :]

    def product_tile(block_now):
        return lax.dot_general(
            weighted,
            block_now,
            (((1,), (1,)), ((), ())),
            precision=lax.Precision.HIGHEST,
            preferred_element_type=jnp.float32,
        )

    def advance(block_now):
        return from_behind(block_now, "tm", -1)

    partials = jnp.zeros((halfway + 1, snap_cols, snap_cols), jnp.float32)
    partials = lax.dynamic_update_index_in_dim(partials, product_tile(snaps), 0, 0)

    def advance_four(step_index, carry):
        block_now, partials = carry
        for offset_step in range(4):
            block_now = advance(block_now)
            partials = lax.dynamic_update_index_in_dim(
                partials, product_tile(block_now), 4 * step_index + offset_step + 1, 0
            )
        return (block_now, partials)

    block_now, partials = lax.fori_loop(0, halfway // 4, advance_four, (snaps, partials))
    offsets = jnp.arange(halfway + 1, dtype=jnp.int32)
    keep_last = jnp.where((offsets == halfway) & (position >= halfway), 0.0, 1.0).astype(
        jnp.float32
    )
    partials = partials * keep_last[:, None, None]
    summed = lax.psum_scatter(partials, "space", scatter_dimension=1, tiled=True)
    padding_up = jnp.zeros((cycle_size - halfway - 1, half_rows, snap_cols), jnp.float32)
    upper = jnp.roll(jnp.concatenate([summed, padding_up], axis=0), position, axis=0)
    keep_mirror = jnp.where(offsets > 0, 1.0, 0.0).astype(jnp.float32)
    flipped = jnp.swapaxes(summed, 1, 2) * keep_mirror[:, None, None]
    padding_down = jnp.zeros((cycle_size - halfway - 1, snap_cols, half_rows), jnp.float32)
    outgoing = jnp.roll(jnp.concatenate([flipped, padding_down], axis=0), position, axis=0)
    incoming = lax.all_to_all(
        lax.all_to_all(outgoing, "tm", split_axis=0, concat_axis=0, tiled=True),
        "space",
        split_axis=1,
        concat_axis=2,
        tiled=True,
    )
    panel = upper + incoming
    return jnp.transpose(panel, (1, 0, 2)).reshape(half_rows, cycle_size * snap_cols)


def solution(mesh):
    return jax.shard_map(
        on_device,
        mesh=mesh,
        in_specs=(P("tm", ("slab", "space")), P(("slab", "space"))),
        out_specs=P(("slab", "tm", "space"), None),
        check_vma=False,
    )
```

profile of v0, /device:TPU:0, one launch (start us, length us, event | category | flops | bytes accessed | tf_op | source)
XLA Modules:
  0.0 76.2 jit_solution(11004154498868069931)
XLA Ops:
  6.5 0.0 copy-start
  6.5 0.0 reduce-scatter.2.cloned.1.call-start
  6.5 6.0 %collective-permute-start = (f32[16,2048]{1,0:T(8,128)}, f32[16,2048]{1,0:T(8,128)S(1)}, u32[]{:S(2)}, u32[]{:S(2)}) collective-permute-start(f32[16,2048]{1,0:T(8,128)} %param.2), channel_id=1, source_target_pairs={{2,0},{4,2},{6,4},{8,6},{10,8},{12,10},{14,12},{0,14},{3,1},{5,3},... | collective-permute-start | bytes 393224 | tf_op jit(solution)/shard_map/while/body/eval_jaxpr/ppermute | solution.py:10
  12.5 1.3 %convolution_bitcast_fusion.4 = f32[1,16,16]{2,1,0:T(8,128)S(1)} fusion(f32[16,2048]{1,0:T(8,128)} %param.2, f32[2048]{0:T(1024)} %param.3), kind=kOutput, calls=%fused_computation.8 | convolution fusion | flops 6324224 | bytes 140288 | tf_op jit(solution)/shard_map/dot_general | solution.py:22
  13.8 0.0 copy-start.1
  13.9 1.7 %collective-permute-done = f32[16,2048]{1,0:T(8,128)S(1)} collective-permute-done((f32[16,2048]{1,0:T(8,128)}, f32[16,2048]{1,0:T(8,128)S(1)}, u32[]{:S(2)}, u32[]{:S(2)}) %collective-permute-start) | collective-permute-done | bytes 131104 | tf_op jit(solution)/shard_map/while/body/eval_jaxpr/ppermute | solution.py:10
  15.6 5.1 %collective-permute-start.1 = (f32[16,2048]{1,0:T(8,128)S(1)}, f32[16,2048]{1,0:T(8,128)S(1)}, u32[]{:S(2)}, u32[]{:S(2)}) collective-permute-start(f32[16,2048]{1,0:T(8,128)S(1)} %collective-permute-done), channel_id=1, source_target_pairs={{2,0},{4,2},{6,4},{8,6},{10,8},{12,10},{14,12},{0,14},{3,1},{5,3},... | collective-permute-start | bytes 393224 | tf_op jit(solution)/shard_map/while/body/eval_jaxpr/ppermute | solution.py:10
  20.7 0.0 copy-done
  20.7 0.0 copy-done.1
  20.7 0.2 fusion.3
  20.9 2.3 %collective-permute-done.1 = f32[16,2048]{1,0:T(8,128)S(1)} collective-permute-done((f32[16,2048]{1,0:T(8,128)S(1)}, f32[16,2048]{1,0:T(8,128)S(1)}, u32[]{:S(2)}, u32[]{:S(2)}) %collective-permute-start.1) | collective-permute-done | bytes 131104 | tf_op jit(solution)/shard_map/while/body/eval_jaxpr/ppermute | solution.py:10
  23.2 5.1 %collective-permute-start.2 = (f32[16,2048]{1,0:T(8,128)S(1)}, f32[16,2048]{1,0:T(8,128)S(1)}, u32[]{:S(2)}, u32[]{:S(2)}) collective-permute-start(f32[16,2048]{1,0:T(8,128)S(1)} %collective-permute-done.1), channel_id=1, source_target_pairs={{2,0},{4,2},{6,4},{8,6},{10,8},{12,10},{14,12},{0,14},{3,1},{5,3},... | collective-permute-start | bytes 393224 | tf_op jit(solution)/shard_map/while/body/eval_jaxpr/ppermute | solution.py:10
  28.3 0.2 fusion.2
  28.6 2.3 %collective-permute-done.2 = f32[16,2048]{1,0:T(8,128)S(1)} collective-permute-done((f32[16,2048]{1,0:T(8,128)S(1)}, f32[16,2048]{1,0:T(8,128)S(1)}, u32[]{:S(2)}, u32[]{:S(2)}) %collective-permute-start.2) | collective-permute-done | bytes 131104 | tf_op jit(solution)/shard_map/while/body/eval_jaxpr/ppermute | solution.py:10
  30.8 5.1 %collective-permute-start.3 = (f32[16,2048]{1,0:T(8,128)S(1)}, f32[16,2048]{1,0:T(8,128)S(1)}, u32[]{:S(2)}, u32[]{:S(2)}) collective-permute-start(f32[16,2048]{1,0:T(8,128)S(1)} %collective-permute-done.2), channel_id=1, source_target_pairs={{2,0},{4,2},{6,4},{8,6},{10,8},{12,10},{14,12},{0,14},{3,1},{5,3},... | collective-permute-start | bytes 393224 | tf_op jit(solution)/shard_map/while/body/eval_jaxpr/ppermute | solution.py:10
  36.0 0.2 fusion.1
  36.2 2.3 %collective-permute-done.3 = f32[16,2048]{1,0:T(8,128)S(1)} collective-permute-done((f32[16,2048]{1,0:T(8,128)S(1)}, f32[16,2048]{1,0:T(8,128)S(1)}, u32[]{:S(2)}, u32[]{:S(2)}) %collective-permute-start.3) | collective-permute-done | bytes 131104 | tf_op jit(solution)/shard_map/while/body/eval_jaxpr/ppermute | solution.py:10
  38.5 0.2 fusion
  38.8 0.8 broadcast_multiply_fusion
  39.5 0.0 reduce-scatter.2.cloned.1.call-update
  39.6 9.4 %reduce-scatter.2.cloned.1.call-done = f32[5,8,16]{2,1,0:T(8,128)} async-done(((f32[5,16,16]{2,1,0:T(8,128)}), f32[5,8,16]{2,1,0:T(8,128)}) %reduce-scatter.2.cloned.1.call-update) | async-done | bytes 2576 | tf_op jit(solution)/shard_map/reduce_scatter | solution.py:51
  49.0 0.8 %multiply_bitcast_fusion = f32[5,16,8]{1,2,0:T(8,128)S(1)} fusion(f32[5,8,16]{2,1,0:T(8,128)} %reduce-scatter.2.cloned.1.call-done, f32[5]{0:T(128)S(1)} %compare_select_fusion), kind=kLoop, calls=%fused_computation.36 | loop fusion | flops 640 | bytes 5140 | tf_op jit(solution)/shard_map/mul | solution.py:55
  49.8 0.1 fusion.22
  49.8 0.1 reshape.16
  49.9 12.0 %all_to_all.23 = f32[8,1,128]{2,1,0:T(1,128)S(1)} all-to-all(f32[8,1,128]{2,1,0:T(1,128)S(1)} %reshape.16), channel_id=1, replica_groups=mesh['slab'=2,'tm'=8,'space'=2] {'tm'}, dimensions={0} | all-to-all | bytes 8192 | tf_op jit(solution)/shard_map/all_to_all | solution.py:59
  61.9 0.5 broadcast.43
  62.4 0.7 reduce
  63.1 0.1 reshape.17
  63.2 0.1 copy.6
  63.3 0.1 reshape.18
  63.4 3.7 %all_to_all.24 = f32[2,1,512]{2,1,0:T(1,128)S(1)} all-to-all(f32[2,1,512]{2,1,0:T(1,128)S(1)} %reshape.18), channel_id=1, replica_groups=mesh['slab'=2,'tm'=8,'space'=2] {'space'}, dimensions={0} | all-to-all | bytes 8192 | tf_op jit(solution)/shard_map/all_to_all | solution.py:58
  67.1 0.7 reduce.1
  67.7 0.1 reshape.19
  67.8 0.1 copy.10
  67.9 0.0 copy-start.2
  67.9 0.1 all_to_all.20
  68.0 0.6 copy-done.2
  68.7 0.7 reshape.15
  (7 shorter events, 0.1 us)
Async XLA Ops:
  6.5 14.1 %copy-start = (f32[16,2048]{1,0:T(8,128)S(1)}, f32[16,2048]{1,0:T(8,128)}, u32[]{:S(2)}) copy-start(f32[16,2048]{1,0:T(8,128)} %param.2) | copy-start | bytes 393220
  6.5 42.5 %reduce-scatter.2.cloned.1.call-start = ((), (), s32[]{:S(2)}) async-start(), calls=%async_computation.3 | async-start | bytes 61440 | tf_op jit(solution)/shard_map/reduce_scatter | solution.py:51
  6.5 9.0 %collective-permute-start = (f32[16,2048]{1,0:T(8,128)}, f32[16,2048]{1,0:T(8,128)S(1)}, u32[]{:S(2)}, u32[]{:S(2)}) collective-permute-start(f32[16,2048]{1,0:T(8,128)} %param.2), channel_id=1, source_target_pairs={{2,0},{4,2},{6,4},{8,6},{10,8},{12,10},{14,12},{0,14},{3,1},{5,3},... | collective-permute-start | bytes 393224 | tf_op jit(solution)/shard_map/while/body/eval_jaxpr/ppermute | solution.py:10
  13.8 6.9 %copy-start.1 = (f32[2048]{0:T(1024)S(1)}, f32[2048]{0:T(1024)}, u32[]{:S(2)}) copy-start(f32[2048]{0:T(1024)} %param.3) | copy-start | bytes 24580
  15.6 7.6 %collective-permute-start.1 = (f32[16,2048]{1,0:T(8,128)S(1)}, f32[16,2048]{1,0:T(8,128)S(1)}, u32[]{:S(2)}, u32[]{:S(2)}) collective-permute-start(f32[16,2048]{1,0:T(8,128)S(1)} %collective-permute-done), channel_id=1, source_target_pairs={{2,0},{4,2},{6,4},{8,6},{10,8},{12,10},{14,12},{0,14},{3,1},{5,3},... | collective-permute-start | bytes 393224 | tf_op jit(solution)/shard_map/while/body/eval_jaxpr/ppermute | solution.py:10
  23.2 7.7 %collective-permute-start.2 = (f32[16,2048]{1,0:T(8,128)S(1)}, f32[16,2048]{1,0:T(8,128)S(1)}, u32[]{:S(2)}, u32[]{:S(2)}) collective-permute-start(f32[16,2048]{1,0:T(8,128)S(1)} %collective-permute-done.1), channel_id=1, source_target_pairs={{2,0},{4,2},{6,4},{8,6},{10,8},{12,10},{14,12},{0,14},{3,1},{5,3},... | collective-permute-start | bytes 393224 | tf_op jit(solution)/shard_map/while/body/eval_jaxpr/ppermute | solution.py:10
  30.8 7.7 %collective-permute-start.3 = (f32[16,2048]{1,0:T(8,128)S(1)}, f32[16,2048]{1,0:T(8,128)S(1)}, u32[]{:S(2)}, u32[]{:S(2)}) collective-permute-start(f32[16,2048]{1,0:T(8,128)S(1)} %collective-permute-done.2), channel_id=1, source_target_pairs={{2,0},{4,2},{6,4},{8,6},{10,8},{12,10},{14,12},{0,14},{3,1},{5,3},... | collective-permute-start | bytes 393224 | tf_op jit(solution)/shard_map/while/body/eval_jaxpr/ppermute | solution.py:10
  67.9 0.7 copy-start.2
Sparse Core Ops, SparseCore 0:
  39.7 9.2 reduce-scatter.1
where the time goes:
time: 76.5 us; the launch traced here: 76.2 us
  starting transfers between devices  21.3 us (28%)
  waiting for transfers between devices  18 us (24%)
  blocking collectives  15.7 us (21%)
  between operations  13.6 us (18%)
  other arithmetic  2.99 us (4%)
  local copies, waits for them, and re-layouts  2.42 us (3%)
  matrix products  2.24 us (3%)
    ppermute x4, starting transfers between devices, from_behind(): return lax.ppermute(block, axis, route)  21.3 us
    all_to_all x1, blocking collectives, on_device(): lax.all_to_all(outgoing, 'tm', split_axis=0, concat_axis=0, tiled=True)  12 us
    reduce_scatter x1, waiting for transfers between devices, on_device(): lax.psum_scatter(partials, 'space', scatter_dimension=1, tiled=True)  9.42 us
    ppermute x4, waiting for transfers between devices, from_behind(): return lax.ppermute(block, axis, route)  8.53 us
    all_to_all x1, blocking collectives, on_device(): lax.all_to_all(lax.all_to_all(outgoing, 'tm', split_axis=0, concat_axis=0...  3.69 us
    dot_general x5, matrix products, product_tile(): lax.dot_general(weighted, block_now, (((1,), (1,)), ((), ())), precision=...  2.24 us
  transfers between devices with their start and end apart: 5, of which 5 were waited for; matrix products, arithmetic and copies ran while one was open for 3% of the time, Pallas kernels for 0%

commit v1 on v0

--- a/solution.py
+++ b/solution.py
@@ -1,7 +1,121 @@
+import functools
+
 import jax
 import jax.numpy as jnp
 from jax import lax
+from jax.experimental import pallas as pl
+from jax.experimental.pallas import tpu as pltpu
 from jax.sharding import PartitionSpec as P
+
+MESH = pl.DeviceIdType.MESH
+LANES = 128
+
+
+def exchange_kernel(n, spaces, snaps_ref, weights_ref, out_ref, block, gram, landed, own_sem, send_one, recv_one, send_two, recv_two):
+    t, s = lax.axis_index("tm"), lax.axis_index("space")
+    me = t * spaces + s
+    everyone = n * spaces
+    depth = snaps_ref.shape[0]
+    cells = snaps_ref.shape[1] // n
+    rows = depth // spaces
+
+    barrier = pltpu.get_barrier_semaphore()
+    for d in range(1, everyone):
+        q = lax.rem(me + d, everyone)
+        pl.semaphore_signal(
+            barrier,
+            inc=1,
+            device_id={"tm": lax.div(q, spaces), "space": lax.rem(q, spaces)},
+            device_id_type=MESH,
+        )
+
+    def columns(owner):
+        return pl.ds(pl.multiple_of(owner * cells, cells), cells)
+
+    my_rows = block.at[pl.ds(pl.multiple_of(t * depth, depth), depth), :]
+    own = pltpu.make_async_copy(snaps_ref.at[:, columns(t)], my_rows, own_sem)
+    own.start()
+    pl.semaphore_wait(barrier, everyone - 1)
+
+    first = []
+    for d in range(1, n):
+        to = lax.rem(t + d, n)
+        copy = pltpu.make_async_remote_copy(
+            src_ref=snaps_ref.at[:, columns(to)],
+            dst_ref=my_rows,
+            send_sem=send_one.at[d],
+            recv_sem=recv_one.at[d],
+            device_id={"tm": to},
+            device_id_type=MESH,
+        )
+        copy.start()
+        first.append(copy)
+    own.wait()
+    for copy in first:
+        copy.wait_recv()
+
+    pieces = cells // LANES
+    weights = weights_ref[pl.ds(t * pieces, pieces), :]
+    data = block[...]
+    weighted = jnp.concatenate(
+        [data[:, k * LANES : (k + 1) * LANES] * weights[k : k + 1, :] for k in range(pieces)], axis=1
+    )
+    gram[...] = lax.dot_general(
+        weighted,
+        data,
+        (((1,), (1,)), ((), ())),
+        precision=lax.Precision.HIGHEST,
+        preferred_element_type=jnp.float32,
+    )
+
+    second = []
+    for d in range(1, everyone):
+        q = lax.rem(me + d, everyone)
+        copy = pltpu.make_async_remote_copy(
+            src_ref=gram.at[pl.ds(pl.multiple_of(q * rows, rows), rows), :],
+            dst_ref=landed.at[d],
+            send_sem=send_two.at[d],
+            recv_sem=recv_two.at[d],
+            device_id={"tm": lax.div(q, spaces), "space": lax.rem(q, spaces)},
+            device_id_type=MESH,
+        )
+        copy.start()
+        second.append(copy)
+    total = gram[pl.ds(pl.multiple_of(me * rows, rows), rows), :]
+    for d, copy in enumerate(second, 1):
+        copy.wait_recv()
+        total = total + landed[d]
+    out_ref[...] = total
+    for copy in first + second:
+        copy.wait_send()
+
+
+def by_exchange(n, spaces, snaps, weights):
+    depth, local = snaps.shape
+    cells = local // n
+    everyone = n * spaces
+    order = n * depth
+    rows = depth // spaces
+    return pl.pallas_call(
+        functools.partial(exchange_kernel, n, spaces),
+        out_shape=jax.ShapeDtypeStruct((rows, order), jnp.float32),
+        in_specs=[pl.BlockSpec(memory_space=pl.ANY), pl.BlockSpec(memory_space=pltpu.VMEM)],
+        out_specs=pl.BlockSpec(memory_space=pltpu.VMEM),
+        scratch_shapes=[
+            pltpu.VMEM((order, cells), jnp.float32),
+            pltpu.VMEM((order, order), jnp.float32),
+            pltpu.VMEM((everyone, rows, order), jnp.float32),
+            pltpu.SemaphoreType.DMA,
+            pltpu.SemaphoreType.DMA((n,)),
+            pltpu.SemaphoreType.DMA((n,)),
+            pltpu.SemaphoreType.DMA((everyone,)),
+            pltpu.SemaphoreType.DMA((everyone,)),
+        ],
+        compiler_params=pltpu.CompilerParams(collective_id=0, has_side_effects=True),
+        cost_estimate=pl.CostEstimate(
+            flops=12 * order * order * cells, bytes_accessed=4 * depth * local, transcendentals=0
+        ),
+    )(snaps, weights.reshape(local // LANES, LANES))
 
 
 def from_behind(block, axis, distance):
@@ -10,7 +124,7 @@
     return lax.ppermute(block, axis, route)
 
 
-def on_device(snaps, weights):
+def by_ring(snaps, weights):
     snap_cols = snaps.shape[0]
     half_rows = snap_cols // 2
     cycle_size = lax.axis_size("tm")
@@ -67,6 +181,14 @@
 
 
 def solution(mesh):
+    n, spaces = mesh.shape["tm"], mesh.shape["space"]
+
+    def on_device(snaps, weights):
+        depth, local = snaps.shape
+        if local % (n * LANES) == 0 and depth % (8 * spaces) == 0:
+            return by_exchange(n, spaces, snaps, weights)
+        return by_ring(snaps, weights)
+
     return jax.shard_map(
         on_device,
         mesh=mesh,

time: 76.5 us -> 19.2 us (0.25)
  starting transfers between devices: 21.3 us -> 0 us
  waiting for transfers between devices: 18 us -> 0 us
  Pallas kernels: 0 us -> 17.7 us
  blocking collectives: 15.7 us -> 0 us
  between operations: 13.6 us -> 0.01 us
  other arithmetic: 2.99 us -> 0 us
  matrix products: 2.24 us -> 0 us
  local copies, waits for them, and re-layouts: 2.42 us -> 1.28 us
    ppermute x4 -> x0, starting transfers between devices: 21.3 us -> none  [from_behind(): return lax.ppermute(block, axis, route)]
    pallas_call x0 -> x1, Pallas kernels: none -> 17.7 us  [by_exchange(): pl.pallas_call(functools.partial(exchange_kernel, n, spaces), out_shape=j...]
    all_to_all x2 -> x0, blocking collectives: 15.7 us -> none  [the longest x1 12 us: on_device(): lax.all_to_all(outgoing, 'tm', split_axis=0, concat_axis=0, tiled=True)]
    reduce_scatter x1 -> x0, waiting for transfers between devices: 9.42 us -> none  [on_device(): lax.psum_scatter(partials, 'space', scatter_dimension=1, tiled=True)]
    ppermute x4 -> x0, waiting for transfers between devices: 8.53 us -> none  [from_behind(): return lax.ppermute(block, axis, route)]
    dot_general x5 -> x0, matrix products: 2.24 us -> none  [product_tile(): lax.dot_general(weighted, block_now, (((1,), (1,)), ((), ())), precision=...]
    mul x2 -> x0, other arithmetic: 1.55 us -> none  [the longest x1 0.8 us: on_device(): flipped = jnp.swapaxes(summed, 1, 2) * keep_mirror[:, None, None]]
    all_to_all x2 -> x0, other arithmetic: 1.32 us -> none  [the longest x1 0.67 us: on_device(): lax.all_to_all(lax.all_to_all(outgoing, 'tm', split_axis=0, concat_axis=0...]
  transfers between devices with their start and end apart: 5 -> 0, of which waited for: 5 -> 0; matrix products, arithmetic and copies ran while one was open for 3% -> 0% of each run, Pallas kernels for 0% -> 0%
where the time goes in v1:
time: 19.2 us; the launch traced here: 18.9 us
  Pallas kernels  17.7 us (92%)
  local copies, waits for them, and re-layouts  1.28 us (7%)
    pallas_call x1, Pallas kernels, by_exchange(): pl.pallas_call(functools.partial(exchange_kernel, n, spaces), out_shape=j...  17.7 us
    unnamed x1, local copies, waits for them, and re-layouts  1.28 us

profile of v1, /device:TPU:0, one launch (start us, length us, event | category | flops | bytes accessed | tf_op | source)
XLA Modules:
  0.0 18.9 jit_solution(12341278578102328278)
XLA Ops:
  0.0 17.7 %shard_map.28 = f32[8,128]{1,0:T(8,128)} custom-call(f32[16,2048]{1,0:T(8,128)} %snaps_ref.1, f32[16,128]{1,0:T(8,128)} %bitcast.1), custom_call_target="tpu_custom_call" | custom-call | flops 50331648 | bytes 131072 | tf_op jit(solution)/shard_map/pallas_call | solution.py:99
  17.7 1.3 %copy.4 = f32[8,128]{1,0:T(8,128)} copy(f32[8,128]{1,0:T(8,128)} %shard_map.28) | data formatting | bytes 8192

commit v2 on v0

--- a/solution.py
+++ b/solution.py
@@ -1,7 +1,173 @@
+import functools
+
 import jax
 import jax.numpy as jnp
 from jax import lax
+from jax.experimental import pallas as pl
+from jax.experimental.pallas import tpu as pltpu
 from jax.sharding import PartitionSpec as P
+
+MESH = pl.DeviceIdType.MESH
+LANES = 128
+
+
+def exchange_kernel(
+    n, spaces, makers, snaps_ref, weights_ref, out_ref, block, scale, gram, landed,
+    own_sem, ready, send_one, recv_one, send_two, recv_two,
+):
+    t, s = lax.axis_index("tm"), lax.axis_index("space")
+    me = t * spaces + s
+    everyone, every_maker = n * spaces, makers * spaces
+    depth = snaps_ref.shape[0]
+    cells = snaps_ref.shape[1] // makers
+    rows = depth // spaces
+    makes = t < makers
+
+    def device(q):
+        return {"tm": q // spaces, "space": q % spaces}
+
+    def columns(k):
+        return pl.ds(k * cells, cells)
+
+    barrier = pltpu.get_barrier_semaphore()
+    for q in range(everyone):
+
+        @pl.when(makes & (me != q))
+        def _():
+            pl.semaphore_signal(barrier, inc=1, device_id=device(q), device_id_type=MESH)
+
+    my_rows = block.at[pl.ds(pl.multiple_of(t * depth, depth), depth), :]
+    own_columns = pl.ds(pl.multiple_of(lax.rem(t, makers) * cells, cells), cells)
+    own = pltpu.make_async_copy(snaps_ref.at[:, own_columns], my_rows, own_sem.at[0])
+    load = pltpu.make_async_copy(weights_ref, scale, own_sem.at[1])
+
+    @pl.when(makes)
+    def _():
+        own.start()
+        load.start()
+
+    pl.semaphore_wait(barrier, jnp.where(makes, every_maker - 1, every_maker))
+
+    def first(k):
+        return pltpu.make_async_remote_copy(
+            src_ref=snaps_ref.at[:, columns(k)],
+            dst_ref=my_rows,
+            send_sem=send_one.at[k],
+            recv_sem=recv_one.at[lax.rem(t - k + n, n)],
+            device_id={"tm": k},
+            device_id_type=MESH,
+        )
+
+    for k in range(makers):
+
+        @pl.when(t != k)
+        def _():
+            first(k).start()
+
+    for k in range(makers):
+        for other in range(1, spaces):
+            pl.semaphore_signal(
+                ready,
+                inc=1,
+                device_id={"tm": k, "space": lax.rem(s + other, spaces)},
+                device_id_type=MESH,
+            )
+
+    def second(q):
+        return pltpu.make_async_remote_copy(
+            src_ref=gram.at[pl.ds(q * rows, rows), :],
+            dst_ref=landed.at[me],
+            send_sem=send_two.at[q],
+            recv_sem=recv_two.at[me],
+            device_id=device(q),
+            device_id_type=MESH,
+        )
+
+    @pl.when(makes)
+    def _():
+        own.wait()
+        load.wait()
+        for d in range(1, n):
+            source = lax.rem(t + d, n)
+            theirs = block.at[pl.ds(pl.multiple_of(source * depth, depth), depth), :]
+            pltpu.make_async_copy(theirs, theirs, recv_one.at[d]).wait()
+        pieces = cells // LANES
+        weights = scale[pl.ds(t * pieces, pieces), :]
+        data = block[...]
+        weighted = jnp.concatenate(
+            [data[:, k * LANES : (k + 1) * LANES] * weights[k : k + 1, :] for k in range(pieces)],
+            axis=1,
+        )
+        gram[...] = lax.dot_general(
+            weighted,
+            data,
+            (((1,), (1,)), ((), ())),
+            precision=lax.Precision.HIGHEST,
+            preferred_element_type=jnp.float32,
+        )
+        pl.semaphore_wait(ready, (spaces - 1) * n)
+        for q in range(everyone):
+
+            @pl.when(me != q)
+            def _():
+                second(q).start()
+
+        landed[me] = gram[pl.ds(pl.multiple_of(me * rows, rows), rows), :]
+
+    for m in range(every_maker):
+
+        @pl.when(me != m)
+        def _():
+            pltpu.make_async_copy(landed.at[m], landed.at[m], recv_two.at[m]).wait()
+
+    total = landed[0]
+    for m in range(1, every_maker):
+        total = total + landed[m]
+    out_ref[...] = total
+
+    for k in range(makers):
+
+        @pl.when(t != k)
+        def _():
+            first(k).wait_send()
+
+    @pl.when(makes)
+    def _():
+        for q in range(everyone):
+
+            @pl.when(me != q)
+            def _():
+                second(q).wait_send()
+
+
+def by_exchange(n, spaces, makers, snaps, weights):
+    depth, local = snaps.shape
+    cells = local // makers
+    everyone, every_maker = n * spaces, makers * spaces
+    order = n * depth
+    rows = depth // spaces
+    return pl.pallas_call(
+        functools.partial(exchange_kernel, n, spaces, makers),
+        out_shape=jax.ShapeDtypeStruct((rows, order), jnp.float32),
+        in_specs=[pl.BlockSpec(memory_space=pl.ANY)] * 2,
+        out_specs=pl.BlockSpec(memory_space=pltpu.VMEM),
+        scratch_shapes=[
+            pltpu.VMEM((order, cells), jnp.float32),
+            pltpu.VMEM((local // LANES, LANES), jnp.float32),
+            pltpu.VMEM((order, order), jnp.float32),
+            pltpu.VMEM((every_maker, rows, order), jnp.float32),
+            pltpu.SemaphoreType.DMA((2,)),
+            pltpu.SemaphoreType.REGULAR,
+            pltpu.SemaphoreType.DMA((makers,)),
+            pltpu.SemaphoreType.DMA((n,)),
+            pltpu.SemaphoreType.DMA((everyone,)),
+            pltpu.SemaphoreType.DMA((every_maker,)),
+        ],
+        compiler_params=pltpu.CompilerParams(collective_id=0, has_side_effects=True),
+        cost_estimate=pl.CostEstimate(
+            flops=12 * order * order * cells, bytes_accessed=4 * depth * local, transcendentals=0
+        ),
+    )(snaps, weights.reshape(local // LANES, LANES))
 
 
 def from_behind(block, axis, distance):
@@ -10,7 +176,7 @@
     return lax.ppermute(block, axis, route)
 
 
-def on_device(snaps, weights):
+def by_ring(snaps, weights):
     snap_cols = snaps.shape[0]
     half_rows = snap_cols // 2
     cycle_size = lax.axis_size("tm")
@@ -67,6 +233,15 @@
 
 
 def solution(mesh):
+    n, spaces = mesh.shape["tm"], mesh.shape["space"]
+    makers = max(n // 2, 1)
+
+    def on_device(snaps, weights):
+        depth, local = snaps.shape
+        if local % (makers * LANES) == 0 and depth % (8 * spaces) == 0:
+            return by_exchange(n, spaces, makers, snaps, weights)
+        return by_ring(snaps, weights)
+
     return jax.shard_map(
         on_device,
         mesh=mesh,

time: 76.5 us -> 18.2 us (0.24)
  starting transfers between devices: 21.3 us -> 0 us
  waiting for transfers between devices: 18 us -> 0 us
  Pallas kernels: 0 us -> 16.7 us
  blocking collectives: 15.7 us -> 0 us
  between operations: 13.6 us -> 0.01 us
  other arithmetic: 2.99 us -> 0 us
  matrix products: 2.24 us -> 0 us
  local copies, waits for them, and re-layouts: 2.42 us -> 1.28 us
    ppermute x4 -> x0, starting transfers between devices: 21.3 us -> none  [from_behind(): return lax.ppermute(block, axis, route)]
    pallas_call x0 -> x1, Pallas kernels: none -> 16.7 us  [by_exchange(): pl.pallas_call(functools.partial(exchange_kernel, n, spaces, makers), out...]
    all_to_all x2 -> x0, blocking collectives: 15.7 us -> none  [the longest x1 12 us: on_device(): lax.all_to_all(outgoing, 'tm', split_axis=0, concat_axis=0, tiled=True)]
    reduce_scatter x1 -> x0, waiting for transfers between devices: 9.42 us -> none  [on_device(): lax.psum_scatter(partials, 'space', scatter_dimension=1, tiled=True)]
    ppermute x4 -> x0, waiting for transfers between devices: 8.53 us -> none  [from_behind(): return lax.ppermute(block, axis, route)]
    dot_general x5 -> x0, matrix products: 2.24 us -> none  [product_tile(): lax.dot_general(weighted, block_now, (((1,), (1,)), ((), ())), precision=...]
    mul x2 -> x0, other arithmetic: 1.55 us -> none  [the longest x1 0.8 us: on_device(): flipped = jnp.swapaxes(summed, 1, 2) * keep_mirror[:, None, None]]
    all_to_all x2 -> x0, other arithmetic: 1.32 us -> none  [the longest x1 0.67 us: on_device(): lax.all_to_all(lax.all_to_all(outgoing, 'tm', split_axis=0, concat_axis=0...]
  transfers between devices with their start and end apart: 5 -> 0, of which waited for: 5 -> 0; matrix products, arithmetic and copies ran while one was open for 3% -> 0% of each run, Pallas kernels for 0% -> 0%
where the time goes in v2:
time: 18.2 us; the launch traced here: 18 us
  Pallas kernels  16.7 us (92%)
  local copies, waits for them, and re-layouts  1.28 us (7%)
    pallas_call x1, Pallas kernels, by_exchange(): pl.pallas_call(functools.partial(exchange_kernel, n, spaces, makers), out...  16.7 us
    unnamed x1, local copies, waits for them, and re-layouts  1.28 us

profile of v2, /device:TPU:0, one launch (start us, length us, event | category | flops | bytes accessed | tf_op | source)
XLA Modules:
  0.0 18.0 jit_solution(7429028040824367975)
XLA Ops:
  0.0 16.7 %shard_map.28 = f32[8,128]{1,0:T(8,128)} custom-call(f32[16,2048]{1,0:T(8,128)} %snaps_ref.1, f32[16,128]{1,0:T(8,128)} %bitcast.1), custom_call_target="tpu_custom_call" | custom-call | flops 100663296 | bytes 131072 | tf_op jit(solution)/shard_map/pallas_call | solution.py:149
  16.7 1.3 %copy.4 = f32[8,128]{1,0:T(8,128)} copy(f32[8,128]{1,0:T(8,128)} %shard_map.28) | data formatting | bytes 8192

commit v3 on v2

--- a/solution.py
+++ b/solution.py
@@ -11,15 +11,25 @@
 LANES = 128
 
 
+def shares_of(n, pieces):
+    makers = n // 2 + 1
+    return tuple((pieces + k) // makers for k in range(makers))
+
+
+def order_of(makers):
+    return list(range(makers))[1::2][::-1] + list(range(makers))[0::2][::-1]
+
+
 def exchange_kernel(
-    n, spaces, makers, snaps_ref, weights_ref, out_ref, block, scale, gram, landed,
+    n, spaces, shares, snaps_ref, weights_ref, landed, block, scale, gram,
     own_sem, ready, send_one, recv_one, send_two, recv_two,
 ):
     t, s = lax.axis_index("tm"), lax.axis_index("space")
     me = t * spaces + s
+    makers = len(shares)
+    starts = [sum(shares[:k]) for k in range(makers)]
     everyone, every_maker = n * spaces, makers * spaces
     depth = snaps_ref.shape[0]
-    cells = snaps_ref.shape[1] // makers
     rows = depth // spaces
     makes = t < makers
 
@@ -27,7 +37,15 @@
         return {"tm": q // spaces, "space": q % spaces}
 
     def columns(k):
-        return pl.ds(k * cells, cells)
+        return pl.ds(starts[k] * LANES, shares[k] * LANES)
+
+    def by_share(work):
+        for share in sorted(set(shares)):
+            mine = [k for k in range(makers) if shares[k] == share]
+            is_mine = functools.reduce(jnp.logical_or, [t == k for k in mine])
+            pl.when(is_mine)(functools.partial(work, share))
+
+    start = sum(jnp.where(t == k, starts[k], 0) for k in range(makers))
 
     barrier = pltpu.get_barrier_semaphore()
     for q in range(everyone):
@@ -36,14 +54,18 @@
         def _():
             pl.semaphore_signal(barrier, inc=1, device_id=device(q), device_id_type=MESH)
 
-    my_rows = block.at[pl.ds(pl.multiple_of(t * depth, depth), depth), :]
-    own_columns = pl.ds(pl.multiple_of(lax.rem(t, makers) * cells, cells), cells)
-    own = pltpu.make_async_copy(snaps_ref.at[:, own_columns], my_rows, own_sem.at[0])
+    def rows_of(source, share):
+        return block.at[pl.ds(pl.multiple_of(source * depth, depth), depth), pl.ds(0, share * LANES)]
+
+    def own(share):
+        columns = pl.ds(pl.multiple_of(start * LANES, LANES), share * LANES)
+        return pltpu.make_async_copy(snaps_ref.at[:, columns], rows_of(t, share), own_sem.at[0])
+
     load = pltpu.make_async_copy(weights_ref, scale, own_sem.at[1])
 
-    @pl.when(makes)
-    def _():
-        own.start()
+    @by_share
+    def _(share):
+        own(share).start()
         load.start()
 
     pl.semaphore_wait(barrier, jnp.where(makes, every_maker - 1, every_maker))
@@ -51,14 +73,14 @@
     def first(k):
         return pltpu.make_async_remote_copy(
             src_ref=snaps_ref.at[:, columns(k)],
-            dst_ref=my_rows,
+            dst_ref=rows_of(t, shares[k]),
             send_sem=send_one.at[k],
             recv_sem=recv_one.at[lax.rem(t - k + n, n)],
             device_id={"tm": k},
             device_id_type=MESH,
         )
 
-    for k in range(makers):
+    for k in order_of(makers):
 
         @pl.when(t != k)
         def _():
@@ -83,19 +105,17 @@
             device_id_type=MESH,
         )
 
-    @pl.when(makes)
-    def _():
-        own.wait()
+    @by_share
+    def _(share):
+        own(share).wait()
         load.wait()
         for d in range(1, n):
-            source = lax.rem(t + d, n)
-            theirs = block.at[pl.ds(pl.multiple_of(source * depth, depth), depth), :]
+            theirs = rows_of(lax.rem(t + d, n), share)
             pltpu.make_async_copy(theirs, theirs, recv_one.at[d]).wait()
-        pieces = cells // LANES
-        weights = scale[pl.ds(t * pieces, pieces), :]
-        data = block[...]
+        weights = scale[pl.ds(start, share), :]
+        data = block[:, 0 : share * LANES]
         weighted = jnp.concatenate(
-            [data[:, k * LANES : (k + 1) * LANES] * weights[k : k + 1, :] for k in range(pieces)],
+            [data[:, k * LANES : (k + 1) * LANES] * weights[k : k + 1, :] for k in range(share)],
             axis=1,
         )
         gram[...] = lax.dot_general(
@@ -105,6 +125,9 @@
             precision=lax.Precision.HIGHEST,
             preferred_element_type=jnp.float32,
         )
+
+    @pl.when(makes)
+    def _():
         pl.semaphore_wait(ready, (spaces - 1) * n)
         for q in range(everyone):
 
@@ -112,18 +135,15 @@
             def _():
                 second(q).start()
 
-        landed[me] = gram[pl.ds(pl.multiple_of(me * rows, rows), rows), :]
+        keep = pltpu.make_async_copy(gram.at[pl.ds(pl.multiple_of(me * rows, rows), rows), :], landed.at[me], own_sem.at[0])
+        keep.start()
+        keep.wait()
 
     for m in range(every_maker):
 
         @pl.when(me != m)
         def _():
             pltpu.make_async_copy(landed.at[m], landed.at[m], recv_two.at[m]).wait()
-
-    total = landed[0]
-    for m in range(1, every_maker):
-        total = total + landed[m]
-    out_ref[...] = total
 
     for k in range(makers):
 
@@ -140,22 +160,21 @@
                 second(q).wait_send()
 
 
-def by_exchange(n, spaces, makers, snaps, weights):
+def by_exchange(n, spaces, shares, snaps, weights):
     depth, local = snaps.shape
-    cells = local // makers
+    makers, cells = len(shares), max(shares) * LANES
     everyone, every_maker = n * spaces, makers * spaces
     order = n * depth
     rows = depth // spaces
-    return pl.pallas_call(
-        functools.partial(exchange_kernel, n, spaces, makers),
-        out_shape=jax.ShapeDtypeStruct((rows, order), jnp.float32),
+    tiles = pl.pallas_call(
+        functools.partial(exchange_kernel, n, spaces, shares),
+        out_shape=jax.ShapeDtypeStruct((every_maker, rows, order), jnp.float32),
         in_specs=[pl.BlockSpec(memory_space=pl.ANY)] * 2,
-        out_specs=pl.BlockSpec(memory_space=pltpu.VMEM),
+        out_specs=pl.BlockSpec(memory_space=pl.ANY),
         scratch_shapes=[
             pltpu.VMEM((order, cells), jnp.float32),
             pltpu.VMEM((local // LANES, LANES), jnp.float32),
             pltpu.VMEM((order, order), jnp.float32),
-            pltpu.VMEM((every_maker, rows, order), jnp.float32),
             pltpu.SemaphoreType.DMA((2,)),
             pltpu.SemaphoreType.REGULAR,
             pltpu.SemaphoreType.DMA((makers,)),
@@ -168,6 +187,7 @@
             flops=12 * order * order * cells, bytes_accessed=4 * depth * local, transcendentals=0
         ),
     )(snaps, weights.reshape(local // LANES, LANES))
+    return jnp.sum(tiles, axis=0)
 
 
 def from_behind(block, axis, distance):
@@ -234,12 +254,12 @@
 
 def solution(mesh):
     n, spaces = mesh.shape["tm"], mesh.shape["space"]
-    makers = max(n // 2, 1)
 
     def on_device(snaps, weights):
         depth, local = snaps.shape
-        if local % (makers * LANES) == 0 and depth % (8 * spaces) == 0:
-            return by_exchange(n, spaces, makers, snaps, weights)
+        shares = shares_of(n, local // LANES)
+        if local % LANES == 0 and min(shares) > 0 and depth % (8 * spaces) == 0:
+            return by_exchange(n, spaces, shares, snaps, weights)
         return by_ring(snaps, weights)
 
     return jax.shard_map(

time: 18.2 us -> 15.3 us (0.84)
  Pallas kernels: 16.7 us -> 13.7 us
  other arithmetic: 0 us -> 1.38 us
  local copies, waits for them, and re-layouts: 1.28 us -> 0 us
    pallas_call x1, Pallas kernels: 16.7 us -> 13.7 us  [by_exchange(): pl.pallas_call(functools.partial(exchange_kernel, n, spaces, shares), out...]
    reduce_sum x0 -> x1, other arithmetic: none -> 1.38 us  [by_exchange(): return jnp.sum(tiles, axis=0)]
    unnamed x1 -> x0, local copies, waits for them, and re-layouts: 1.28 us -> none
where the time goes in v3:
time: 15.3 us; the launch traced here: 15.1 us
  Pallas kernels  13.7 us (90%)
  other arithmetic  1.38 us (9%)
    pallas_call x1, Pallas kernels, by_exchange(): pl.pallas_call(functools.partial(exchange_kernel, n, spaces, shares), out...  13.7 us
    reduce_sum x1, other arithmetic, by_exchange(): return jnp.sum(tiles, axis=0)  1.38 us

profile of v3, /device:TPU:0, one launch (start us, length us, event | category | flops | bytes accessed | tf_op | source)
XLA Modules:
  0.0 15.1 jit_solution(5817312438535813286)
XLA Ops:
  0.0 13.7 %shard_map.28 = f32[10,8,128]{2,1,0:T(8,128)} custom-call(f32[16,2048]{1,0:T(8,128)} %snaps_ref.1, f32[16,128]{1,0:T(8,128)} %bitcast.1), custom_call_target="tpu_custom_call" | custom-call | flops 100663296 | bytes 131072 | tf_op jit(solution)/shard_map/pallas_call | solution.py:169
  13.8 1.4 %reduce_sum.9 = f32[8,128]{1,0:T(8,128)} reduce(f32[10,8,128]{2,1,0:T(8,128)} %shard_map.28, f32[]{:T(128)} %constant.0.clone.1), dimensions={0}, to_apply=%region_0.0 | reduce | flops 9216 | bytes 45060 | tf_op jit(solution)/shard_map/reduce_sum | solution.py:190

commit v4 on v3

--- a/solution.py
+++ b/solution.py
@@ -21,7 +21,7 @@
 
 
 def exchange_kernel(
-    n, spaces, shares, snaps_ref, weights_ref, landed, block, scale, gram,
+    n, spaces, shares, snaps_ref, weights_ref, landed, block, stage, scale, gram,
     own_sem, ready, send_one, recv_one, send_two, recv_two,
 ):
     t, s = lax.axis_index("tm"), lax.axis_index("space")
@@ -48,31 +48,12 @@
     start = sum(jnp.where(t == k, starts[k], 0) for k in range(makers))
 
     barrier = pltpu.get_barrier_semaphore()
-    for q in range(everyone):
-
-        @pl.when(makes & (me != q))
-        def _():
-            pl.semaphore_signal(barrier, inc=1, device_id=device(q), device_id_type=MESH)
-
     def rows_of(source, share):
         return block.at[pl.ds(pl.multiple_of(source * depth, depth), depth), pl.ds(0, share * LANES)]
 
-    def own(share):
-        columns = pl.ds(pl.multiple_of(start * LANES, LANES), share * LANES)
-        return pltpu.make_async_copy(snaps_ref.at[:, columns], rows_of(t, share), own_sem.at[0])
-
-    load = pltpu.make_async_copy(weights_ref, scale, own_sem.at[1])
-
-    @by_share
-    def _(share):
-        own(share).start()
-        load.start()
-
-    pl.semaphore_wait(barrier, jnp.where(makes, every_maker - 1, every_maker))
-
-    def first(k):
+    def first(k, source=snaps_ref):
         return pltpu.make_async_remote_copy(
-            src_ref=snaps_ref.at[:, columns(k)],
+            src_ref=source.at[:, columns(k)],
             dst_ref=rows_of(t, shares[k]),
             send_sem=send_one.at[k],
             recv_sem=recv_one.at[lax.rem(t - k + n, n)],
@@ -80,11 +61,44 @@
             device_id_type=MESH,
         )
 
-    for k in order_of(makers):
-
-        @pl.when(t != k)
-        def _():
+    @pl.when(jnp.logical_not(makes))
+    def _():
+        pl.semaphore_wait(barrier, every_maker)
+        for k in order_of(makers):
             first(k).start()
+
+    @pl.when(makes)
+    def _():
+        for q in range(everyone):
+
+            @pl.when(me != q)
+            def _():
+                pl.semaphore_signal(barrier, inc=1, device_id=device(q), device_id_type=MESH)
+
+    def own(share):
+        columns = pl.ds(pl.multiple_of(start * LANES, LANES), share * LANES)
+        return pltpu.make_async_copy(snaps_ref.at[:, columns], rows_of(t, share), own_sem.at[0])
+
+    load = pltpu.make_async_copy(weights_ref, scale, own_sem.at[1])
+    fetch = pltpu.make_async_copy(snaps_ref, stage, own_sem.at[2])
+
+    @by_share
+    def _(share):
+        fetch.start()
+        own(share).start()
+        load.start()
+
+
+    @pl.when(makes)
+    def _():
+        pl.semaphore_wait(barrier, every_maker - 1)
+        fetch.wait()
+        for k in order_of(makers):
+
+            @pl.when(t != k)
+            def _():
+                first(k, stage).start()
+
 
     for k in range(makers):
         for other in range(1, spaces):
@@ -126,18 +140,19 @@
             preferred_element_type=jnp.float32,
         )
 
-    @pl.when(makes)
-    def _():
+    keep = pltpu.make_async_copy(
+        gram.at[pl.ds(pl.multiple_of(me * rows, rows), rows), :], landed.at[jnp.where(makes, me, 0)], own_sem.at[0]
+    )
+
+    @pl.when(makes)
+    def _():
+        keep.start()
         pl.semaphore_wait(ready, (spaces - 1) * n)
         for q in range(everyone):
 
             @pl.when(me != q)
             def _():
                 second(q).start()
-
-        keep = pltpu.make_async_copy(gram.at[pl.ds(pl.multiple_of(me * rows, rows), rows), :], landed.at[me], own_sem.at[0])
-        keep.start()
-        keep.wait()
 
     for m in range(every_maker):
 
@@ -153,6 +168,7 @@
 
     @pl.when(makes)
     def _():
+        keep.wait()
         for q in range(everyone):
 
             @pl.when(me != q)
@@ -173,9 +189,10 @@
         out_specs=pl.BlockSpec(memory_space=pl.ANY),
         scratch_shapes=[
             pltpu.VMEM((order, cells), jnp.float32),
+            pltpu.VMEM((depth, local), jnp.float32),
             pltpu.VMEM((local // LANES, LANES), jnp.float32),
             pltpu.VMEM((order, order), jnp.float32),
-            pltpu.SemaphoreType.DMA((2,)),
+            pltpu.SemaphoreType.DMA((3,)),
             pltpu.SemaphoreType.REGULAR,
             pltpu.SemaphoreType.DMA((makers,)),
             pltpu.SemaphoreType.DMA((n,)),

time: 15.3 us -> 15.3 us (level)
  no operation moved by 1% of the time
where the time goes in v4:
time: 15.3 us; the launch traced here: 15.1 us
  Pallas kernels  13.8 us (90%)
  other arithmetic  1.38 us (9%)
    pallas_call x1, Pallas kernels, by_exchange(): pl.pallas_call(functools.partial(exchange_kernel, n, spaces, shares), out...  13.8 us
    reduce_sum x1, other arithmetic, by_exchange(): return jnp.sum(tiles, axis=0)  1.38 us

profile of v4, /device:TPU:0, one launch (start us, length us, event | category | flops | bytes accessed | tf_op | source)
XLA Modules:
  0.0 15.1 jit_solution(9923506406882086825)
XLA Ops:
  0.0 13.8 %shard_map.28 = f32[10,8,128]{2,1,0:T(8,128)} custom-call(f32[16,2048]{1,0:T(8,128)} %snaps_ref.1, f32[16,128]{1,0:T(8,128)} %bitcast.1), custom_call_target="tpu_custom_call" | custom-call | flops 100663296 | bytes 131072 | tf_op jit(solution)/shard_map/pallas_call | solution.py:185
  13.8 1.4 %reduce_sum.9 = f32[8,128]{1,0:T(8,128)} reduce(f32[10,8,128]{2,1,0:T(8,128)} %shard_map.28, f32[]{:T(128)} %constant.0.clone.1), dimensions={0}, to_apply=%region_0.0 | reduce | flops 9216 | bytes 45060 | tf_op jit(solution)/shard_map/reduce_sum | solution.py:207

commit v5 on v4

--- a/solution.py
+++ b/solution.py
@@ -13,7 +13,9 @@
 
 def shares_of(n, pieces):
     makers = n // 2 + 1
-    return tuple((pieces + k) // makers for k in range(makers))
+    last = min(pieces, pieces // makers + 2)
+    others = [(pieces - last + k) // (makers - 1) for k in range(makers - 1)]
+    return (*reversed(others), last)
 
 
 def order_of(makers):

time: 15.3 us -> 15.1 us (0.987)
  Pallas kernels: 13.8 us -> 13.5 us
    pallas_call x1, Pallas kernels: 13.8 us -> 13.5 us  [by_exchange(): pl.pallas_call(functools.partial(exchange_kernel, n, spaces, shares), out...]
where the time goes in v5:
time: 15.1 us; the launch traced here: 14.9 us
  Pallas kernels  13.5 us (89%)
  other arithmetic  1.38 us (9%)
    pallas_call x1, Pallas kernels, by_exchange(): pl.pallas_call(functools.partial(exchange_kernel, n, spaces, shares), out...  13.5 us
    reduce_sum x1, other arithmetic, by_exchange(): return jnp.sum(tiles, axis=0)  1.38 us

profile of v5, /device:TPU:0, one launch (start us, length us, event | category | flops | bytes accessed | tf_op | source)
XLA Modules:
  0.0 14.9 jit_solution(16960444029343431569)
XLA Ops:
  0.0 13.5 %shard_map.28 = f32[10,8,128]{2,1,0:T(8,128)} custom-call(f32[16,2048]{1,0:T(8,128)} %snaps_ref.1, f32[16,128]{1,0:T(8,128)} %bitcast.1), custom_call_target="tpu_custom_call" | custom-call | flops 125829120 | bytes 131072 | tf_op jit(solution)/shard_map/pallas_call | solution.py:187
  13.5 1.4 %reduce_sum.9 = f32[8,128]{1,0:T(8,128)} reduce(f32[10,8,128]{2,1,0:T(8,128)} %shard_map.28, f32[]{:T(128)} %constant.0.clone.1), dimensions={0}, to_apply=%region_0.0 | reduce | flops 9216 | bytes 45060 | tf_op jit(solution)/shard_map/reduce_sum | solution.py:209

commit v6 on v5

--- a/solution.py
+++ b/solution.py
@@ -67,7 +67,9 @@
     def _():
         pl.semaphore_wait(barrier, every_maker)
         for k in order_of(makers):
-            first(k).start()
+            pl.when(s == 0)(first(k).start)
+        for k in (*range(makers - 1, 0, -2), *range(makers - 2, 0, -2), 0):
+            pl.when(s > 0)(first(k).start)
 
     @pl.when(makes)
     def _():

time: 15.1 us -> 15.1 us (level)
  no operation moved by 1% of the time
where the time goes in v6:
time: 15.1 us; the launch traced here: 14.9 us
  Pallas kernels  13.5 us (89%)
  other arithmetic  1.38 us (9%)
    pallas_call x1, Pallas kernels, by_exchange(): pl.pallas_call(functools.partial(exchange_kernel, n, spaces, shares), out...  13.5 us
    reduce_sum x1, other arithmetic, by_exchange(): return jnp.sum(tiles, axis=0)  1.38 us

profile of v6, /device:TPU:0, one launch (start us, length us, event | category | flops | bytes accessed | tf_op | source)
XLA Modules:
  0.0 14.9 jit_solution(9421294720980551819)
XLA Ops:
  0.0 13.5 %shard_map.28 = f32[10,8,128]{2,1,0:T(8,128)} custom-call(f32[16,2048]{1,0:T(8,128)} %snaps_ref.1, f32[16,128]{1,0:T(8,128)} %bitcast.1), custom_call_target="tpu_custom_call" | custom-call | flops 125829120 | bytes 131072 | tf_op jit(solution)/shard_map/pallas_call | solution.py:189
  13.5 1.4 %reduce_sum.9 = f32[8,128]{1,0:T(8,128)} reduce(f32[10,8,128]{2,1,0:T(8,128)} %shard_map.28, f32[]{:T(128)} %constant.0.clone.1), dimensions={0}, to_apply=%region_0.0 | reduce | flops 9216 | bytes 45060 | tf_op jit(solution)/shard_map/reduce_sum | solution.py:211
